TPU v7x, 256 devices: a whole 4x4x8 slice. The times are simulated.
256 devices in a mesh: gx: 16 (over z, core), gy: 4 (over y), gz: 4 (over x).
Axes of the slice: x: 4, y: 4, z: 8, core: 2. Of those that a mesh axis runs over, the one named last changes fastest.
Arguments:
- basis: float32 [32, 2097152], P(None, ('gx', 'gy', 'gz')), may hold values from -5.5 to 5.5
- sigma: float32 [32], replicated, may hold values from 1 to 8
- snapshots: float32 [64, 2097152], P(None, ('gx', 'gy', 'gz')), may hold values from -200 to 200
Outputs:
- modes: float32 [32, 2097152], P(None, ('gx', 'gy', 'gz'))
- values: float32 [32], replicated
All inputs are finite; a program needn't handle non-finite values.
Results may differ from a plain program's by a relative error of at most 0.00016.
Values sent between devices are 32-bit elements; how exact they have to be, the bound alone decides.
A program may use at most 64 MiB of HBM per device.

v0:
```python
import functools

import jax
import jax.numpy as jnp
from jax import lax
from jax.experimental import pallas as pl
from jax.experimental.pallas import tpu as pltpu
from jax.sharding import PartitionSpec as P

AXES = ("gx", "gy", "gz")
HIGH = lax.Precision.HIGHEST
K, NEW = 32, 64

def dot(a, b): return jnp.dot(a, b, precision=HIGH, preferred_element_type=jnp.float32)
def dot_t(a, b): return lax.dot_general(a, b, (((1,), (1,)), ((), ())), precision=HIGH, preferred_element_type=jnp.float32)

def eliminate(N, U):
    nb = N.shape[0] // 8
    Nb = [N[8*i:8*i+8] for i in range(nb)]
    Ub = [U[8*i:8*i+8] for i in range(nb)]
    row = lax.broadcasted_iota(jnp.int32, (8, 128), 0)
    L = U.shape[1]
    def wide(x, width):
        return x[:, :width] if width <= 128 else jnp.concatenate([x] * (width // 128), axis=1)
    out = []
    for kb in range(nb):
        X = {}
        for j in range(8):
            for i in range(kb, nb):
                X[j, i] = jnp.broadcast_to(Nb[i][:, 8*kb+j:8*kb+j+1], (8, 128))
        scale = jnp.ones((8, 128), jnp.float32)
        for r in range(0, 8, 2):
            spread = lambda x, s: jnp.broadcast_to(x[s:s+1], (8, x.shape[1]))
            a = spread(X[r, kb], r); b = spread(X[r+1, kb], r); c = spread(X[r+1, kb], r+1)
            det = a*c - b*b
            rdet = 1.0 / det
            ra = 1.0 / a
            f1 = {}; f2 = {}
            for i in range(kb, nb):
                f1[i] = (c*X[r, i] - b*X[r+1, i]) * rdet
                f2[i] = (a*X[r+1, i] - b*X[r, i]) * rdet
                if i == kb:
                    f1[i] = jnp.where(row > r+1, f1[i], jnp.where(row == r+1, b*ra, 0.0))
                    f2[i] = jnp.where(row > r+1, f2[i], 0.0)
            for j in range(r+2, 8):
                xa = spread(X[j, kb], r); xb = spread(X[j, kb], r+1)
                for i in range(kb, nb):
                    X[j, i] = X[j, i] - f1[i]*xa - f2[i]*xb
            na = spread(Nb[kb], r); nbb = spread(Nb[kb], r+1)
            ua = spread(Ub[kb], r); ub = spread(Ub[kb], r+1)
            for i in range(kb, nb):
                if kb < nb-1:
                    w = Nb[i].shape[1]
                    Nb[i] = Nb[i] - wide(f1[i], w)*na - wide(f2[i], w)*nbb
                Ub[i] = Ub[i] - wide(f1[i], L)*ua - wide(f2[i], L)*ub
            scale = jnp.where(row == r, lax.rsqrt(a), jnp.where(row == r+1, lax.rsqrt(det*ra), scale))
        out.append(Ub[kb] * wide(scale, L))
    return jnp.concatenate(out, axis=0)

def dense(gbb, f, gss, sigma_row):
    ft = f.T
    t = dot(gbb, f)
    c = 2.0*f - t
    ct = 2.0*ft - dot(ft, gbb)
    h = dot(gbb, c) - f
    gram = gss + dot(jnp.concatenate([ct, -ft], 1), jnp.concatenate([h, c], 0))
    eye = lax.broadcasted_iota(jnp.int32, (K, K), 0) == lax.broadcasted_iota(jnp.int32, (K, K), 1)
    eye2 = lax.broadcasted_iota(jnp.int32, (NEW, NEW), 0) == lax.broadcasted_iota(jnp.int32, (NEW, NEW), 1)
    tau = jnp.sum(c*c, keepdims=True).reshape(1,1) + jnp.sum(jnp.where(eye2, gss, 0.0), keepdims=True).reshape(1,1) + jnp.sum(sigma_row*sigma_row, keepdims=True).reshape(1,1)
    rt = 1.0 / tau
    rs = lax.rsqrt(tau)
    sig2 = jnp.where(eye, sigma_row*sigma_row, 0.0)
    p = (sig2 + dot_t(c, c)) * rt
    cu = c
    c = c*rs; ct = ct*rs; gram = gram*rt
    cg = dot(c, gram); cgt = dot(gram, ct); g2 = dot(gram, gram)
    z32 = jnp.zeros((K, 32), jnp.float32); z64 = jnp.zeros((NEW, 32), jnp.float32)
    top = jnp.concatenate([p, c, z32, p, cg, z32], 1)
    bot = jnp.concatenate([cgt, gram, z64, cgt, g2, z64], 1)
    W = jnp.concatenate([top, bot], 0)
    VZ = top
    for step in range(4):
        V = VZ[:, :96]; Z = VZ[:, 128:224]
        N = dot_t(Z, V)
        VZ = eliminate(N, dot(V, W) if step < 3 else VZ)
    Y = VZ[:, :128]
    P = Y[:, :32]; w = Y[:, 32:96]
    Z = jnp.concatenate([P, dot(w, gram), z32], 1)
    N = dot_t(Z, Y)
    YS = dot(Y[:, :96], W[:, 128:])
    pb = P - dot(w, ct)
    U = jnp.concatenate([pb, w*rs, z32, Y, YS], 1)
    U = eliminate(N, U)
    ritz = jnp.sum(U[:, 128:224] * U[:, 256:352], axis=1, keepdims=True)
    values = jnp.sqrt(ritz * tau)
    return U[:, :128], values


CHUNK = 2048


def gram_kernel(na, ny, nz, basis_hbm, snap_hbm, total_ref, split_hbm,
                basis_v, snap_v, split_v, packed, parts, mine, others, gathered,
                load_sems, store_sem, send_sems, recv_sems):
    x, y, z = lax.axis_index("gx"), lax.axis_index("gy"), lax.axis_index("gz")
    count = ny * nz
    cols = basis_v.shape[1]
    chunks = cols // CHUNK
    loads = []
    for i in range(chunks):
        at = pl.ds(i * CHUNK, CHUNK)
        loads.append((
            pltpu.make_async_copy(basis_hbm.at[:, at], basis_v.at[:, at], load_sems.at[0, i]),
            pltpu.make_async_copy(snap_hbm.at[:, at], snap_v.at[:, at], load_sems.at[1, i]),
        ))
        for copy in loads[-1]:
            copy.start()

    barrier = pltpu.get_barrier_semaphore()
    for d in range(1, na):
        pl.semaphore_signal(barrier, inc=1, device_id={"gx": lax.rem(x + d, na)}, device_id_type=pl.DeviceIdType.MESH)
    def place(d):
        return {"gy": lax.rem(y + d // nz, ny), "gz": lax.rem(z + d % nz, nz)}
    for d in range(1, count):
        pl.semaphore_signal(barrier, inc=1, device_id=place(d), device_id_type=pl.DeviceIdType.MESH)

    full = None
    for i in range(chunks):
        for copy in loads[i]:
            copy.wait()
        at = slice(i * CHUNK, (i + 1) * CHUNK)
        for ref, low in ((basis_v, 0), (snap_v, K)):
            value = ref[:, at]
            high = value.astype(jnp.bfloat16)
            rest = (value - high.astype(jnp.float32)).astype(jnp.bfloat16)
            split_v[low:low + value.shape[0], at] = high
            split_v[K + NEW + low:K + NEW + low + value.shape[0], at] = rest
        pair = split_v[:, at]
        term = lax.dot_general(pair, pair, (((1,), (1,)), ((), ())), preferred_element_type=jnp.float32)
        full = term if full is None else full + term
    store = pltpu.make_async_copy(split_v, split_hbm, store_sem)
    store.start()
    half = K + NEW
    gram = (full[:half, :half] + full[half:, half:]) + (full[half:, :half] + full[:half, half:])
    gap = jnp.zeros((K, 128 - half), jnp.float32)
    upper = jnp.concatenate([gram[:K], gap], axis=1)
    lower = jnp.concatenate([gram[K:2 * K, K:], gram[2 * K:, K:]], axis=1)
    rows = packed.shape[1]
    both = jnp.concatenate([upper, lower], axis=0)
    for i in range(na):
        packed[i] = both[i * rows:(i + 1) * rows]

    pl.semaphore_wait(barrier, na - 1 + count - 1)

    def send(phase, source, target, device):
        copy = pltpu.make_async_remote_copy(
            src_ref=source, dst_ref=target, send_sem=send_sems.at[phase], recv_sem=recv_sems.at[phase],
            device_id=device, device_id_type=pl.DeviceIdType.MESH)
        copy.start()

    def arrive(phase, ref):
        pltpu.make_async_copy(ref, ref, recv_sems.at[phase]).wait()

    def sent(phase, ref):
        pltpu.make_async_copy(ref, ref, send_sems.at[phase]).wait()

    for d in range(1, na):
        to = lax.rem(x + d, na)
        send(0, packed.at[to], parts.at[d - 1], {"gx": to})
    arrive(0, parts)
    value = packed[x]
    for d in range(na - 1):
        value = value + parts[d]
    mine[...] = value

    here = y * nz + z
    for d in range(1, count):
        send(1, mine, others.at[here], place(d))
    others[here] = value
    arrive(1, others.at[pl.ds(0, count - 1)])
    value = others[0]
    for d in range(1, count):
        value = value + others[d]
    gathered[x] = value

    for d in range(1, na):
        send(2, gathered.at[x], gathered.at[x], {"gx": lax.rem(x + d, na)})
    arrive(2, gathered.at[pl.ds(0, na - 1)])
    for i in range(na):
        total_ref[i] = gathered[i]
    sent(0, parts)
    sent(1, others.at[pl.ds(0, count - 1)])
    sent(2, gathered.at[pl.ds(0, na - 1)])
    store.wait()


def update_kernel(rows, total_ref, sigma_ref, split_hbm, modes_ref, values_ref, split_v, sem):
    cols = split_v.shape[1]
    copy = pltpu.make_async_copy(split_hbm, split_v, sem)
    copy.start()
    total = total_ref[...] * (1.0 / rows)
    upper, lower = total[:K], total[K:]
    gss = jnp.concatenate([lower[:, :NEW], lower[:, NEW:]], axis=0)
    coef, values = dense(upper[:, :K], upper[:, K:K + NEW], gss, sigma_ref[...])
    eye = lax.broadcasted_iota(jnp.int32, (K, K), 0) == lax.broadcasted_iota(jnp.int32, (K, K), 1)
    values_ref[...] = jnp.sum(jnp.where(eye, values, 0.0), axis=0, keepdims=True)
    coef = coef[:, :K + NEW]
    high = coef.astype(jnp.bfloat16).astype(jnp.float32)
    rest = coef - high
    left = jnp.concatenate([
        jnp.concatenate([high, high], axis=1), jnp.concatenate([rest, rest], axis=1)], axis=0).astype(jnp.bfloat16)
    copy.wait()
    for i in range(cols // CHUNK):
        at = slice(i * CHUNK, (i + 1) * CHUNK)
        both = jnp.dot(left, split_v[:, at], preferred_element_type=jnp.float32)
        modes_ref[:, at] = both[:K] + both[K:]


def per_device(basis, sigma, snapshots):
    na, ny, nz = (lax.axis_size(a) for a in AXES)
    cols = basis.shape[1]
    rows = cols * na * ny * nz
    piece = 2 * K // na
    vmem = pl.BlockSpec(memory_space=pltpu.VMEM)
    hbm = pl.BlockSpec(memory_space=pl.ANY)
    count = ny * nz
    total, split = pl.pallas_call(
        functools.partial(gram_kernel, na, ny, nz),
        out_shape=(jax.ShapeDtypeStruct((na, piece, 128), jnp.float32),
                   jax.ShapeDtypeStruct((2 * (K + NEW), cols), jnp.bfloat16)),
        in_specs=[hbm, hbm],
        out_specs=(vmem, hbm),
        scratch_shapes=[
            pltpu.VMEM((K, cols), jnp.float32),
            pltpu.VMEM((NEW, cols), jnp.float32),
            pltpu.VMEM((2 * (K + NEW), cols), jnp.bfloat16),
            pltpu.VMEM((na, piece, 128), jnp.float32),
            pltpu.VMEM((na - 1, piece, 128), jnp.float32),
            pltpu.VMEM((piece, 128), jnp.float32),
            pltpu.VMEM((count, piece, 128), jnp.float32),
            pltpu.VMEM((na, piece, 128), jnp.float32),
            pltpu.SemaphoreType.DMA((2, cols // CHUNK)),
            pltpu.SemaphoreType.DMA,
            pltpu.SemaphoreType.DMA((3,)),
            pltpu.SemaphoreType.DMA((3,)),
        ],
        compiler_params=pltpu.CompilerParams(
            collective_id=0, has_side_effects=True, vmem_limit_bytes=32 * 1024 * 1024),
        name="gram_reduce",
    )(basis, snapshots)
    modes, values = pl.pallas_call(
        functools.partial(update_kernel, rows),
        out_shape=(jax.ShapeDtypeStruct((K, cols), jnp.float32),
                   jax.ShapeDtypeStruct((1, K), jnp.float32)),
        in_specs=[vmem, vmem, hbm],
        out_specs=(vmem, vmem),
        scratch_shapes=[pltpu.VMEM((2 * (K + NEW), cols), jnp.bfloat16), pltpu.SemaphoreType.DMA],
        compiler_params=pltpu.CompilerParams(vmem_limit_bytes=32 * 1024 * 1024),
        name="modes_update",
    )(total.reshape(2 * K, 128), sigma.reshape(1, K), split)
    return modes, values.reshape(K)


def solution(mesh):
    placed = (P(None, AXES), P(), P(None, AXES))
    return jax.shard_map(
        per_device, mesh=mesh, in_specs=placed, out_specs=(P(None, AXES), P()), check_vma=False)
```

profile of v0, /device:TPU:1, one launch (start us, length us, event | category | flops | bytes accessed | tf_op | source)
XLA Modules:
  0.0 36.7 jit_solution(6777643261954677194)
XLA Ops:
  0.6 0.0 copy-start.2
  0.6 0.0 copy-start
  0.6 1.6 %copy-done = f32[64,8192]{1,0:T(8,128)S(1)} copy-done((f32[64,8192]{1,0:T(8,128)S(1)}, f32[64,8192]{1,0:T(8,128)}, u32[]{:S(2)}) %copy-start) | copy-done | bytes 2097176
  2.2 0.0 copy-start.1
  2.2 1.2 %copy-done.1 = f32[32,8192]{1,0:T(8,128)S(1)} copy-done((f32[32,8192]{1,0:T(8,128)S(1)}, f32[32,8192]{1,0:T(8,128)}, u32[]{:S(2)}) %copy-start.1) | copy-done | bytes 1048600
  3.5 25.5 %gram_reduce.1 = (f32[16,4,128]{2,1,0:T(4,128)S(1)}, bf16[192,8192]{1,0:T(8,128)(2,1)S(1)}) custom-call(f32[32,8192]{1,0:T(8,128)S(1)} %copy-done.1, f32[64,8192]{1,0:T(8,128)S(1)} %copy-done), custom_call_target="tpu_custom_call" | custom-call | tf_op jit(solution)/shard_map/gram_reduce/pallas_call | solution.py:227
  29.0 0.0 copy-done.2
  29.0 7.7 %modes_update.1 = (f32[32,8192]{1,0:T(8,128)}, f32[1,32]{1,0:T(1,128)}) custom-call(f32[64,128]{1,0:T(8,128)S(1)} %bitcast.3, f32[1,32]{1,0:T(1,128)S(1)} %bitcast.4, bf16[192,8192]{1,0:T(8,128)(2,1)S(1)} %get-tuple-element.7.split_hbm), custom_call_target="tpu_custom_call" | custom-call | tf_op jit(solution)/shard_map/modes_update/pallas_call | solution.py:251
Async XLA Ops:
  0.6 28.4 %copy-start.2 = (f32[32]{0:T(128)S(1)}, f32[32]{0:T(128)}, u32[]{:S(2)}) copy-start(f32[32]{0:T(128)} %param.4) | copy-start | bytes 388
  0.6 1.6 %copy-start = (f32[64,8192]{1,0:T(8,128)S(1)}, f32[64,8192]{1,0:T(8,128)}, u32[]{:S(2)}) copy-start(f32[64,8192]{1,0:T(8,128)} %snap_hbm.1) | copy-start | bytes 6291460
  2.2 1.2 %copy-start.1 = (f32[32,8192]{1,0:T(8,128)S(1)}, f32[32,8192]{1,0:T(8,128)}, u32[]{:S(2)}) copy-start(f32[32,8192]{1,0:T(8,128)} %basis_hbm.1) | copy-start | bytes 3145732
where the time goes:
time: 36.9 us; the launch traced here: 36.7 us
  Pallas kernels  33.2 us (90%)
  local copies, waits for them, and re-layouts  2.82 us (8%)
  between operations  0.66 us (2%)
    pallas_call x1, Pallas kernels, per_device(): pl.pallas_call(functools.partial(gram_kernel, na, ny, nz), out_shape=(jax...  25.5 us
    pallas_call x1, Pallas kernels, per_device(): pl.pallas_call(functools.partial(update_kernel, rows), out_shape=(jax.Sha...  7.72 us
    unnamed x6, local copies, waits for them, and re-layouts  2.82 us

commit v1 on v0

--- a/solution.py
+++ b/solution.py
@@ -8,6 +8,7 @@
 from jax.sharding import PartitionSpec as P
 
 AXES = ("gx", "gy", "gz")
+MESH = pl.DeviceIdType.MESH
 HIGH = lax.Precision.HIGHEST
 K, NEW = 32, 64
 
@@ -97,36 +98,19 @@
 
 
 CHUNK = 2048
-
-
-def gram_kernel(na, ny, nz, basis_hbm, snap_hbm, total_ref, split_hbm,
-                basis_v, snap_v, split_v, packed, parts, mine, others, gathered,
-                load_sems, store_sem, send_sems, recv_sems):
-    x, y, z = lax.axis_index("gx"), lax.axis_index("gy"), lax.axis_index("gz")
-    count = ny * nz
-    cols = basis_v.shape[1]
-    chunks = cols // CHUNK
-    loads = []
-    for i in range(chunks):
-        at = pl.ds(i * CHUNK, CHUNK)
-        loads.append((
-            pltpu.make_async_copy(basis_hbm.at[:, at], basis_v.at[:, at], load_sems.at[0, i]),
-            pltpu.make_async_copy(snap_hbm.at[:, at], snap_v.at[:, at], load_sems.at[1, i]),
-        ))
-        for copy in loads[-1]:
-            copy.start()
-
-    barrier = pltpu.get_barrier_semaphore()
-    for d in range(1, na):
-        pl.semaphore_signal(barrier, inc=1, device_id={"gx": lax.rem(x + d, na)}, device_id_type=pl.DeviceIdType.MESH)
-    def place(d):
-        return {"gy": lax.rem(y + d // nz, ny), "gz": lax.rem(z + d % nz, nz)}
-    for d in range(1, count):
-        pl.semaphore_signal(barrier, inc=1, device_id=place(d), device_id_type=pl.DeviceIdType.MESH)
-
+STACK = 2 * (K + NEW)
+
+
+def tree_sum(values):
+    while len(values) > 1:
+        values = [a + b for a, b in zip(values[::2], values[1::2])] + values[len(values) // 2 * 2:]
+    return values[0]
+
+
+def split_gram(loads, basis_v, snap_v, split_v):
     full = None
-    for i in range(chunks):
-        for copy in loads[i]:
+    for i, pair in enumerate(loads):
+        for copy in pair:
             copy.wait()
         at = slice(i * CHUNK, (i + 1) * CHUNK)
         for ref, low in ((basis_v, 0), (snap_v, K)):
@@ -135,28 +119,59 @@
             rest = (value - high.astype(jnp.float32)).astype(jnp.bfloat16)
             split_v[low:low + value.shape[0], at] = high
             split_v[K + NEW + low:K + NEW + low + value.shape[0], at] = rest
-        pair = split_v[:, at]
-        term = lax.dot_general(pair, pair, (((1,), (1,)), ((), ())), preferred_element_type=jnp.float32)
+        both = split_v[:, at]
+        term = lax.dot_general(both, both, (((1,), (1,)), ((), ())), preferred_element_type=jnp.float32)
         full = term if full is None else full + term
+    half = K + NEW
+    return (full[:half, :half] + full[half:, half:]) + (full[half:, :half] + full[:half, half:])
+
+
+def gram_kernel(na, ny, nz, basis_hbm, snap_hbm, total_ref, split_hbm,
+                basis_v, snap_v, split_v, packed, partner, chip, s1a, s1b, s2a, s2b, mids, gathered,
+                load_sems, store_sem, send_sems, recv_sems):
+    x, y, z = lax.axis_index("gx"), lax.axis_index("gy"), lax.axis_index("gz")
+    deep = na // 2
+    level, core = x // 2, lax.rem(x, 2)
+    cols = basis_v.shape[1]
+    loads = []
+    for i in range(cols // CHUNK):
+        at = pl.ds(i * CHUNK, CHUNK)
+        loads.append((
+            pltpu.make_async_copy(basis_hbm.at[:, at], basis_v.at[:, at], load_sems.at[0, i]),
+            pltpu.make_async_copy(snap_hbm.at[:, at], snap_v.at[:, at], load_sems.at[1, i]),
+        ))
+        for copy in loads[-1]:
+            copy.start()
+
+    def hops(d, n):
+        return min(d, n - d)
+
+    other = {"gx": x + 1 - 2 * core}
+    plane = [(hops(dy, ny) + hops(dz, nz), {"gy": lax.rem(y + dy, ny), "gz": lax.rem(z + dz, nz)})
+             for dy in range(ny) for dz in range(nz) if dy or dz]
+    line = [(hops(d, deep), {"gx": lax.rem(level + d, deep) * 2 + core}) for d in range(1, deep)]
+    barrier = pltpu.get_barrier_semaphore()
+    for device in [other] + [d for _, d in plane + line]:
+        pl.semaphore_signal(barrier, inc=1, device_id=device, device_id_type=MESH)
+
+    gram = split_gram(loads, basis_v, snap_v, split_v)
     store = pltpu.make_async_copy(split_v, split_hbm, store_sem)
     store.start()
     half = K + NEW
-    gram = (full[:half, :half] + full[half:, half:]) + (full[half:, :half] + full[:half, half:])
     gap = jnp.zeros((K, 128 - half), jnp.float32)
     upper = jnp.concatenate([gram[:K], gap], axis=1)
     lower = jnp.concatenate([gram[K:2 * K, K:], gram[2 * K:, K:]], axis=1)
-    rows = packed.shape[1]
-    both = jnp.concatenate([upper, lower], axis=0)
-    for i in range(na):
-        packed[i] = both[i * rows:(i + 1) * rows]
-
-    pl.semaphore_wait(barrier, na - 1 + count - 1)
+    rows = K // 2
+    for i in range(2):
+        packed[0, i] = upper[i * rows:(i + 1) * rows]
+        packed[1, i] = lower[i * rows:(i + 1) * rows]
+
+    pl.semaphore_wait(barrier, 1 + len(plane) + len(line))
 
     def send(phase, source, target, device):
-        copy = pltpu.make_async_remote_copy(
+        pltpu.make_async_remote_copy(
             src_ref=source, dst_ref=target, send_sem=send_sems.at[phase], recv_sem=recv_sems.at[phase],
-            device_id=device, device_id_type=pl.DeviceIdType.MESH)
-        copy.start()
+            device_id=device, device_id_type=MESH).start()
 
     def arrive(phase, ref):
         pltpu.make_async_copy(ref, ref, recv_sems.at[phase]).wait()
@@ -164,40 +179,51 @@
     def sent(phase, ref):
         pltpu.make_async_copy(ref, ref, send_sems.at[phase]).wait()
 
-    for d in range(1, na):
-        to = lax.rem(x + d, na)
-        send(0, packed.at[to], parts.at[d - 1], {"gx": to})
-    arrive(0, parts)
-    value = packed[x]
-    for d in range(na - 1):
-        value = value + parts[d]
-    mine[...] = value
-
     here = y * nz + z
-    for d in range(1, count):
-        send(1, mine, others.at[here], place(d))
-    others[here] = value
-    arrive(1, others.at[pl.ds(0, count - 1)])
-    value = others[0]
-    for d in range(1, count):
-        value = value + others[d]
-    gathered[x] = value
-
-    for d in range(1, na):
-        send(2, gathered.at[x], gathered.at[x], {"gx": lax.rem(x + d, na)})
-    arrive(2, gathered.at[pl.ds(0, na - 1)])
-    for i in range(na):
-        total_ref[i] = gathered[i]
-    sent(0, parts)
-    sent(1, others.at[pl.ds(0, count - 1)])
-    sent(2, gathered.at[pl.ds(0, na - 1)])
+    some_plane, some_line = pl.ds(0, len(plane)), pl.ds(0, len(line))
+    send(0, packed.at[1 - core], partner, other)
+    arrive(0, partner)
+    for i in range(2):
+        chip[i] = packed[core, i] + partner[i]
+    for far, which, device in sorted(
+            [(far, 0, device) for far, device in plane] + [(far, 1, device) for far, device in line],
+            key=lambda entry: -entry[0]):
+        if which == 0:
+            send(1, chip.at[0], s1a.at[here], device)
+        else:
+            send(2, chip.at[1], s1b.at[level], device)
+    s1a[here] = chip[0]
+    s1b[level] = chip[1]
+    arrive(2, s1b.at[some_line])
+    mids[1] = tree_sum([s1b[i] for i in range(deep)])
+    for far, device in sorted(plane, key=lambda entry: -entry[0]):
+        send(3, mids.at[1], s2b.at[here], device)
+    s2b[here] = mids[1]
+    arrive(1, s1a.at[some_plane])
+    mids[0] = tree_sum([s1a[i] for i in range(ny * nz)])
+    for far, device in sorted(line, key=lambda entry: -entry[0]):
+        send(4, mids.at[0], s2a.at[level], device)
+    s2a[level] = mids[0]
+    arrive(4, s2a.at[some_line])
+    gathered[core, 0] = tree_sum([s2a[i] for i in range(deep)])
+    arrive(3, s2b.at[some_plane])
+    gathered[core, 1] = tree_sum([s2b[i] for i in range(ny * nz)])
+    send(5, gathered.at[core], gathered.at[core], other)
+    arrive(5, gathered.at[1 - core])
+    total_ref[...] = gathered[...]
+    sent(0, partner)
+    sent(1, s1a.at[some_plane])
+    sent(2, s1b.at[some_line])
+    sent(3, s2b.at[some_plane])
+    sent(4, s2a.at[some_line])
+    sent(5, partner)
     store.wait()
 
 
-def update_kernel(rows, total_ref, sigma_ref, split_hbm, modes_ref, values_ref, split_v, sem):
+def update_kernel(rows, total_ref, sigma_ref, split_hbm, modes_hbm, values_ref, split_v, modes_v, load_sem, out_sems):
     cols = split_v.shape[1]
-    copy = pltpu.make_async_copy(split_hbm, split_v, sem)
-    copy.start()
+    load = pltpu.make_async_copy(split_hbm, split_v, load_sem)
+    load.start()
     total = total_ref[...] * (1.0 / rows)
     upper, lower = total[:K], total[K:]
     gss = jnp.concatenate([lower[:, :NEW], lower[:, NEW:]], axis=0)
@@ -209,43 +235,47 @@
     rest = coef - high
     left = jnp.concatenate([
         jnp.concatenate([high, high], axis=1), jnp.concatenate([rest, rest], axis=1)], axis=0).astype(jnp.bfloat16)
-    copy.wait()
+    load.wait()
+    copies = []
     for i in range(cols // CHUNK):
         at = slice(i * CHUNK, (i + 1) * CHUNK)
         both = jnp.dot(left, split_v[:, at], preferred_element_type=jnp.float32)
-        modes_ref[:, at] = both[:K] + both[K:]
+        modes_v[:, at] = both[:K] + both[K:]
+        span = pl.ds(i * CHUNK, CHUNK)
+        copies.append(pltpu.make_async_copy(modes_v.at[:, span], modes_hbm.at[:, span], out_sems.at[i]))
+        copies[-1].start()
+    for copy in copies:
+        copy.wait()
 
 
 def per_device(basis, sigma, snapshots):
     na, ny, nz = (lax.axis_size(a) for a in AXES)
     cols = basis.shape[1]
     rows = cols * na * ny * nz
-    piece = 2 * K // na
     vmem = pl.BlockSpec(memory_space=pltpu.VMEM)
-    hbm = pl.BlockSpec(memory_space=pl.ANY)
-    count = ny * nz
+    hbm = pl.BlockSpec(memory_space=pltpu.HBM)
+    quarter = (K // 2, 128)
+    def slots(*count):
+        return pltpu.VMEM(count + quarter, jnp.float32)
     total, split = pl.pallas_call(
         functools.partial(gram_kernel, na, ny, nz),
-        out_shape=(jax.ShapeDtypeStruct((na, piece, 128), jnp.float32),
-                   jax.ShapeDtypeStruct((2 * (K + NEW), cols), jnp.bfloat16)),
+        out_shape=(jax.ShapeDtypeStruct((2, 2) + quarter, jnp.float32),
+                   jax.ShapeDtypeStruct((STACK, cols), jnp.bfloat16)),
         in_specs=[hbm, hbm],
         out_specs=(vmem, hbm),
         scratch_shapes=[
             pltpu.VMEM((K, cols), jnp.float32),
             pltpu.VMEM((NEW, cols), jnp.float32),
-            pltpu.VMEM((2 * (K + NEW), cols), jnp.bfloat16),
-            pltpu.VMEM((na, piece, 128), jnp.float32),
-            pltpu.VMEM((na - 1, piece, 128), jnp.float32),
-            pltpu.VMEM((piece, 128), jnp.float32),
-            pltpu.VMEM((count, piece, 128), jnp.float32),
-            pltpu.VMEM((na, piece, 128), jnp.float32),
+            pltpu.VMEM((STACK, cols), jnp.bfloat16),
+            slots(2, 2), slots(2), slots(2),
+            slots(ny * nz), slots(na // 2), slots(na // 2), slots(ny * nz), slots(2), slots(2, 2),
             pltpu.SemaphoreType.DMA((2, cols // CHUNK)),
             pltpu.SemaphoreType.DMA,
-            pltpu.SemaphoreType.DMA((3,)),
-            pltpu.SemaphoreType.DMA((3,)),
+            pltpu.SemaphoreType.DMA((6,)),
+            pltpu.SemaphoreType.DMA((6,)),
         ],
         compiler_params=pltpu.CompilerParams(
-            collective_id=0, has_side_effects=True, vmem_limit_bytes=32 * 1024 * 1024),
+            collective_id=0, has_side_effects=True, vmem_limit_bytes=53 * 1024 * 1024),
         name="gram_reduce",
     )(basis, snapshots)
     modes, values = pl.pallas_call(
@@ -253,9 +283,11 @@
         out_shape=(jax.ShapeDtypeStruct((K, cols), jnp.float32),
                    jax.ShapeDtypeStruct((1, K), jnp.float32)),
         in_specs=[vmem, vmem, hbm],
-        out_specs=(vmem, vmem),
-        scratch_shapes=[pltpu.VMEM((2 * (K + NEW), cols), jnp.bfloat16), pltpu.SemaphoreType.DMA],
-        compiler_params=pltpu.CompilerParams(vmem_limit_bytes=32 * 1024 * 1024),
+        out_specs=(hbm, vmem),
+        scratch_shapes=[
+            pltpu.VMEM((STACK, cols), jnp.bfloat16), pltpu.VMEM((K, cols), jnp.float32),
+            pltpu.SemaphoreType.DMA, pltpu.SemaphoreType.DMA((cols // CHUNK,))],
+        compiler_params=pltpu.CompilerParams(vmem_limit_bytes=53 * 1024 * 1024),
         name="modes_update",
     )(total.reshape(2 * K, 128), sigma.reshape(1, K), split)
     return modes, values.reshape(K)

time: 36.9 us -> 33.2 us (0.90)
  local copies, waits for them, and re-layouts: 2.82 us -> 0.01 us
  Pallas kernels: 33.2 us -> 32.4 us
    unnamed x6 -> x2, local copies, waits for them, and re-layouts: 2.82 us -> 0.01 us
    pallas_call x1, Pallas kernels: 25.5 us -> 23.1 us  [per_device(): pl.pallas_call(functools.partial(gram_kernel, na, ny, nz), out_shape=(jax...]
    pallas_call x1, Pallas kernels: 7.72 us -> 9.34 us  [per_device(): pl.pallas_call(functools.partial(update_kernel, rows), out_shape=(jax.Sha...]
where the time goes in v1:
time: 33.2 us; the launch traced here: 33.1 us
  Pallas kernels  32.4 us (98%)
  between operations  0.65 us (2%)
    pallas_call x1, Pallas kernels, per_device(): pl.pallas_call(functools.partial(gram_kernel, na, ny, nz), out_shape=(jax...  23.1 us
    pallas_call x1, Pallas kernels, per_device(): pl.pallas_call(functools.partial(update_kernel, rows), out_shape=(jax.Sha...  9.34 us

profile of v1, /device:TPU:1, one launch (start us, length us, event | category | flops | bytes accessed | tf_op | source)
XLA Modules:
  0.0 33.1 jit_solution(5003988011106353783)
XLA Ops:
  0.6 0.0 copy-start
  0.6 23.1 %gram_reduce.1 = (f32[2,2,16,128]{3,2,1,0:T(8,128)S(1)}, bf16[192,8192]{1,0:T(8,128)(2,1)}) custom-call(f32[32,8192]{1,0:T(8,128)} %basis_hbm.1, f32[64,8192]{1,0:T(8,128)} %snap_hbm.1), custom_call_target="tpu_custom_call" | custom-call | tf_op jit(solution)/shard_map/gram_reduce/pallas_call | solution.py:260
  23.7 0.0 copy-done
  23.7 9.3 %modes_update.1 = (f32[32,8192]{1,0:T(8,128)}, f32[1,32]{1,0:T(1,128)}) custom-call(f32[64,128]{1,0:T(8,128)S(1)} %bitcast.3, f32[1,32]{1,0:T(1,128)S(1)} %bitcast.4, bf16[192,8192]{1,0:T(8,128)(2,1)} %get-tuple-element.7.split_hbm), custom_call_target="tpu_custom_call" | custom-call | tf_op jit(solution)/shard_map/modes_update/pallas_call | solution.py:281
Async XLA Ops:
  0.6 23.1 %copy-start = (f32[32]{0:T(128)S(1)}, f32[32]{0:T(128)}, u32[]{:S(2)}) copy-start(f32[32]{0:T(128)} %param.4) | copy-start | bytes 388

commit v2 on v1

--- a/solution.py
+++ b/solution.py
@@ -126,9 +126,9 @@
     return (full[:half, :half] + full[half:, half:]) + (full[half:, :half] + full[:half, half:])
 
 
-def gram_kernel(na, ny, nz, basis_hbm, snap_hbm, total_ref, split_hbm,
+def update_kernel(na, ny, nz, basis_hbm, sigma_ref, snap_hbm, modes_ref, values_ref,
                 basis_v, snap_v, split_v, packed, partner, chip, s1a, s1b, s2a, s2b, mids, gathered,
-                load_sems, store_sem, send_sems, recv_sems):
+                load_sems, send_sems, recv_sems):
     x, y, z = lax.axis_index("gx"), lax.axis_index("gy"), lax.axis_index("gz")
     deep = na // 2
     level, core = x // 2, lax.rem(x, 2)
@@ -155,8 +155,6 @@
         pl.semaphore_signal(barrier, inc=1, device_id=device, device_id_type=MESH)
 
     gram = split_gram(loads, basis_v, snap_v, split_v)
-    store = pltpu.make_async_copy(split_v, split_hbm, store_sem)
-    store.start()
     half = K + NEW
     gap = jnp.zeros((K, 128 - half), jnp.float32)
     upper = jnp.concatenate([gram[:K], gap], axis=1)
@@ -210,22 +208,8 @@
     gathered[core, 1] = tree_sum([s2b[i] for i in range(ny * nz)])
     send(5, gathered.at[core], gathered.at[core], other)
     arrive(5, gathered.at[1 - core])
-    total_ref[...] = gathered[...]
-    sent(0, partner)
-    sent(1, s1a.at[some_plane])
-    sent(2, s1b.at[some_line])
-    sent(3, s2b.at[some_plane])
-    sent(4, s2a.at[some_line])
-    sent(5, partner)
-    store.wait()
-
-
-def update_kernel(rows, total_ref, sigma_ref, split_hbm, modes_hbm, values_ref, split_v, modes_v, load_sem, out_sems):
-    cols = split_v.shape[1]
-    load = pltpu.make_async_copy(split_hbm, split_v, load_sem)
-    load.start()
-    total = total_ref[...] * (1.0 / rows)
-    upper, lower = total[:K], total[K:]
+    upper = jnp.concatenate([gathered[0, 0], gathered[0, 1]], axis=0) * (1.0 / (cols * na * ny * nz))
+    lower = jnp.concatenate([gathered[1, 0], gathered[1, 1]], axis=0) * (1.0 / (cols * na * ny * nz))
     gss = jnp.concatenate([lower[:, :NEW], lower[:, NEW:]], axis=0)
     coef, values = dense(upper[:, :K], upper[:, K:K + NEW], gss, sigma_ref[...])
     eye = lax.broadcasted_iota(jnp.int32, (K, K), 0) == lax.broadcasted_iota(jnp.int32, (K, K), 1)
@@ -235,34 +219,32 @@
     rest = coef - high
     left = jnp.concatenate([
         jnp.concatenate([high, high], axis=1), jnp.concatenate([rest, rest], axis=1)], axis=0).astype(jnp.bfloat16)
-    load.wait()
-    copies = []
     for i in range(cols // CHUNK):
         at = slice(i * CHUNK, (i + 1) * CHUNK)
         both = jnp.dot(left, split_v[:, at], preferred_element_type=jnp.float32)
-        modes_v[:, at] = both[:K] + both[K:]
-        span = pl.ds(i * CHUNK, CHUNK)
-        copies.append(pltpu.make_async_copy(modes_v.at[:, span], modes_hbm.at[:, span], out_sems.at[i]))
-        copies[-1].start()
-    for copy in copies:
-        copy.wait()
+        modes_ref[:, at] = both[:K] + both[K:]
+    sent(0, partner)
+    sent(1, s1a.at[some_plane])
+    sent(2, s1b.at[some_line])
+    sent(3, s2b.at[some_plane])
+    sent(4, s2a.at[some_line])
+    sent(5, partner)
 
 
 def per_device(basis, sigma, snapshots):
     na, ny, nz = (lax.axis_size(a) for a in AXES)
     cols = basis.shape[1]
-    rows = cols * na * ny * nz
     vmem = pl.BlockSpec(memory_space=pltpu.VMEM)
     hbm = pl.BlockSpec(memory_space=pltpu.HBM)
     quarter = (K // 2, 128)
     def slots(*count):
         return pltpu.VMEM(count + quarter, jnp.float32)
-    total, split = pl.pallas_call(
-        functools.partial(gram_kernel, na, ny, nz),
-        out_shape=(jax.ShapeDtypeStruct((2, 2) + quarter, jnp.float32),
-                   jax.ShapeDtypeStruct((STACK, cols), jnp.bfloat16)),
-        in_specs=[hbm, hbm],
-        out_specs=(vmem, hbm),
+    modes, values = pl.pallas_call(
+        functools.partial(update_kernel, na, ny, nz),
+        out_shape=(jax.ShapeDtypeStruct((K, cols), jnp.float32),
+                   jax.ShapeDtypeStruct((1, K), jnp.float32)),
+        in_specs=[hbm, vmem, hbm],
+        out_specs=(vmem, vmem),
         scratch_shapes=[
             pltpu.VMEM((K, cols), jnp.float32),
             pltpu.VMEM((NEW, cols), jnp.float32),
@@ -270,26 +252,13 @@
             slots(2, 2), slots(2), slots(2),
             slots(ny * nz), slots(na // 2), slots(na // 2), slots(ny * nz), slots(2), slots(2, 2),
             pltpu.SemaphoreType.DMA((2, cols // CHUNK)),
-            pltpu.SemaphoreType.DMA,
             pltpu.SemaphoreType.DMA((6,)),
             pltpu.SemaphoreType.DMA((6,)),
         ],
         compiler_params=pltpu.CompilerParams(
-            collective_id=0, has_side_effects=True, vmem_limit_bytes=53 * 1024 * 1024),
-        name="gram_reduce",
-    )(basis, snapshots)
-    modes, values = pl.pallas_call(
-        functools.partial(update_kernel, rows),
-        out_shape=(jax.ShapeDtypeStruct((K, cols), jnp.float32),
-                   jax.ShapeDtypeStruct((1, K), jnp.float32)),
-        in_specs=[vmem, vmem, hbm],
-        out_specs=(hbm, vmem),
-        scratch_shapes=[
-            pltpu.VMEM((STACK, cols), jnp.bfloat16), pltpu.VMEM((K, cols), jnp.float32),
-            pltpu.SemaphoreType.DMA, pltpu.SemaphoreType.DMA((cols // CHUNK,))],
-        compiler_params=pltpu.CompilerParams(vmem_limit_bytes=53 * 1024 * 1024),
-        name="modes_update",
-    )(total.reshape(2 * K, 128), sigma.reshape(1, K), split)
+            collective_id=0, has_side_effects=True, vmem_limit_bytes=52 * 1024 * 1024),
+        name="pod_update",
+    )(basis, sigma.reshape(1, K), snapshots)
     return modes, values.reshape(K)
 
 

time: 33.2 us -> 32.3 us (0.973)
  Pallas kernels: 32.4 us -> 29.4 us
  local copies, waits for them, and re-layouts: 0.01 us -> 2.13 us
    pallas_call x2 -> x1, Pallas kernels: 32.4 us -> 29.4 us  [per_device(): pl.pallas_call(functools.partial(update_kernel, na, ny, nz), out_shape=(j...]
    unnamed x2 -> x4, local copies, waits for them, and re-layouts: 0.01 us -> 2.13 us
where the time goes in v2:
time: 32.3 us; the launch traced here: 32.2 us
  Pallas kernels  29.4 us (91%)
  local copies, waits for them, and re-layouts  2.13 us (7%)
  between operations  0.65 us (2%)
    pallas_call x1, Pallas kernels, per_device(): pl.pallas_call(functools.partial(update_kernel, na, ny, nz), out_shape=(j...  29.4 us
    unnamed x4, local copies, waits for them, and re-layouts  2.13 us

profile of v2, /device:TPU:1, one launch (start us, length us, event | category | flops | bytes accessed | tf_op | source)
XLA Modules:
  0.0 32.2 jit_solution(16587791968997331234)
XLA Ops:
  0.6 0.0 copy-start
  0.6 0.6 %copy-done = f32[32]{0:T(128)S(1)} copy-done((f32[32]{0:T(128)S(1)}, f32[32]{0:T(128)}, u32[]{:S(2)}) %copy-start) | copy-done | bytes 152
  1.3 29.4 %pod_update.1 = (f32[32,8192]{1,0:T(8,128)S(1)}, f32[1,32]{1,0:T(1,128)S(1)}) custom-call(f32[32,8192]{1,0:T(8,128)} %basis_hbm.1, f32[1,32]{1,0:T(1,128)S(1)} %bitcast.2, f32[64,8192]{1,0:T(8,128)} %snap_hbm.1), custom_call_target="tpu_custom_call" | custom-call | tf_op jit(solution)/shard_map/pod_update/pallas_call | solution.py:242
  30.7 1.0 %copy.7 = f32[32,8192]{1,0:T(8,128)} copy(f32[32,8192]{1,0:T(8,128)S(1)} %get-tuple-element.8) | data formatting | bytes 2097152
  31.7 0.5 %copy.8 = f32[32]{0:T(128)} copy(f32[32]{0:T(128)S(1)} %bitcast.3) | data formatting | bytes 256
Async XLA Ops:
  0.6 0.7 %copy-start = (f32[32]{0:T(128)S(1)}, f32[32]{0:T(128)}, u32[]{:S(2)}) copy-start(f32[32]{0:T(128)} %param.4) | copy-start | bytes 388

commit v3 on v2

--- a/solution.py
+++ b/solution.py
@@ -23,14 +23,17 @@
     L = U.shape[1]
     def wide(x, width):
         return x[:, :width] if width <= 128 else jnp.concatenate([x] * (width // 128), axis=1)
+    def column_splats(kb, Nb):
+        return {(j, i): jnp.broadcast_to(Nb[i][:, 8*kb+j:8*kb+j+1], (8, 128))
+                for j in range(8) for i in range(kb, nb)}
     out = []
     for kb in range(nb):
-        X = {}
-        for j in range(8):
-            for i in range(kb, nb):
-                X[j, i] = jnp.broadcast_to(Nb[i][:, 8*kb+j:8*kb+j+1], (8, 128))
+        X = ahead if kb else column_splats(0, Nb)
+        ahead = {}
         scale = jnp.ones((8, 128), jnp.float32)
         for r in range(0, 8, 2):
+            if r == 2 and kb < nb-1:
+                ahead = column_splats(kb+1, Nb)
             spread = lambda x, s: jnp.broadcast_to(x[s:s+1], (8, x.shape[1]))
             a = spread(X[r, kb], r); b = spread(X[r+1, kb], r); c = spread(X[r+1, kb], r+1)
             det = a*c - b*b
@@ -47,6 +50,10 @@
                 xa = spread(X[j, kb], r); xb = spread(X[j, kb], r+1)
                 for i in range(kb, nb):
                     X[j, i] = X[j, i] - f1[i]*xa - f2[i]*xb
+            for j in range(8 if ahead else 0):
+                xa = spread(X[r, kb+1], j); xb = spread(X[r+1, kb+1], j)
+                for i in range(kb+1, nb):
+                    ahead[j, i] = ahead[j, i] - f1[i]*xa - f2[i]*xb
             na = spread(Nb[kb], r); nbb = spread(Nb[kb], r+1)
             ua = spread(Ub[kb], r); ub = spread(Ub[kb], r+1)
             for i in range(kb, nb):
@@ -98,6 +105,8 @@
 
 
 CHUNK = 2048
+LOAD = 2048
+PARTS = 4
 STACK = 2 * (K + NEW)
 
 
@@ -112,7 +121,7 @@
     for i, pair in enumerate(loads):
         for copy in pair:
             copy.wait()
-        at = slice(i * CHUNK, (i + 1) * CHUNK)
+        at = slice(i * LOAD, (i + 1) * LOAD)
         for ref, low in ((basis_v, 0), (snap_v, K)):
             value = ref[:, at]
             high = value.astype(jnp.bfloat16)
@@ -126,22 +135,25 @@
     return (full[:half, :half] + full[half:, half:]) + (full[half:, :half] + full[:half, half:])
 
 
-def update_kernel(na, ny, nz, basis_hbm, sigma_ref, snap_hbm, modes_ref, values_ref,
+def update_kernel(na, ny, nz, basis_hbm, sigma_hbm, snap_hbm, modes_ref, values_ref,
                 basis_v, snap_v, split_v, packed, partner, chip, s1a, s1b, s2a, s2b, mids, gathered,
-                load_sems, send_sems, recv_sems):
+                sigma_ref, sigma_sem, load_sems, send_sems, recv_sems):
     x, y, z = lax.axis_index("gx"), lax.axis_index("gy"), lax.axis_index("gz")
     deep = na // 2
     level, core = x // 2, lax.rem(x, 2)
     cols = basis_v.shape[1]
     loads = []
-    for i in range(cols // CHUNK):
-        at = pl.ds(i * CHUNK, CHUNK)
+    for i in range(cols // LOAD):
+        at = pl.ds(i * LOAD, LOAD)
         loads.append((
             pltpu.make_async_copy(basis_hbm.at[:, at], basis_v.at[:, at], load_sems.at[0, i]),
             pltpu.make_async_copy(snap_hbm.at[:, at], snap_v.at[:, at], load_sems.at[1, i]),
         ))
         for copy in loads[-1]:
             copy.start()
+
+    sigma_load = pltpu.make_async_copy(sigma_hbm, sigma_ref, sigma_sem)
+    sigma_load.start()
 
     def hops(d, n):
         return min(d, n - d)
@@ -208,6 +220,7 @@
     gathered[core, 1] = tree_sum([s2b[i] for i in range(ny * nz)])
     send(5, gathered.at[core], gathered.at[core], other)
     arrive(5, gathered.at[1 - core])
+    sigma_load.wait()
     upper = jnp.concatenate([gathered[0, 0], gathered[0, 1]], axis=0) * (1.0 / (cols * na * ny * nz))
     lower = jnp.concatenate([gathered[1, 0], gathered[1, 1]], axis=0) * (1.0 / (cols * na * ny * nz))
     gss = jnp.concatenate([lower[:, :NEW], lower[:, NEW:]], axis=0)
@@ -231,6 +244,19 @@
     sent(5, partner)
 
 
+def finish_kernel(modes_ref, values_ref, modes_hbm, values_hbm, sems):
+    cols = modes_hbm.shape[1]
+    parts = sems.shape[0] - 1
+    copies = [pltpu.make_async_copy(values_ref, values_hbm, sems.at[parts])]
+    copies[0].start()
+    for i in range(parts):
+        at = pl.ds(i * (cols // parts), cols // parts)
+        copies.append(pltpu.make_async_copy(modes_ref.at[:, at], modes_hbm.at[:, at], sems.at[i]))
+        copies[-1].start()
+    for copy in copies:
+        copy.wait()
+
+
 def per_device(basis, sigma, snapshots):
     na, ny, nz = (lax.axis_size(a) for a in AXES)
     cols = basis.shape[1]
@@ -243,7 +269,7 @@
         functools.partial(update_kernel, na, ny, nz),
         out_shape=(jax.ShapeDtypeStruct((K, cols), jnp.float32),
                    jax.ShapeDtypeStruct((1, K), jnp.float32)),
-        in_specs=[hbm, vmem, hbm],
+        in_specs=[hbm, hbm, hbm],
         out_specs=(vmem, vmem),
         scratch_shapes=[
             pltpu.VMEM((K, cols), jnp.float32),
@@ -251,7 +277,9 @@
             pltpu.VMEM((STACK, cols), jnp.bfloat16),
             slots(2, 2), slots(2), slots(2),
             slots(ny * nz), slots(na // 2), slots(na // 2), slots(ny * nz), slots(2), slots(2, 2),
-            pltpu.SemaphoreType.DMA((2, cols // CHUNK)),
+            pltpu.VMEM((1, K), jnp.float32),
+            pltpu.SemaphoreType.DMA,
+            pltpu.SemaphoreType.DMA((2, cols // LOAD)),
             pltpu.SemaphoreType.DMA((6,)),
             pltpu.SemaphoreType.DMA((6,)),
         ],
@@ -259,6 +287,16 @@
             collective_id=0, has_side_effects=True, vmem_limit_bytes=52 * 1024 * 1024),
         name="pod_update",
     )(basis, sigma.reshape(1, K), snapshots)
+    modes, values = pl.pallas_call(
+        finish_kernel,
+        out_shape=(jax.ShapeDtypeStruct((K, cols), jnp.float32),
+                   jax.ShapeDtypeStruct((1, K), jnp.float32)),
+        in_specs=[pl.BlockSpec(memory_space=pl.ANY), vmem],
+        out_specs=(hbm, hbm),
+        scratch_shapes=[pltpu.SemaphoreType.DMA((PARTS + 1,))],
+        compiler_params=pltpu.CompilerParams(vmem_limit_bytes=1024 * 1024),
+        name="write_out",
+    )(modes, values)
     return modes, values.reshape(K)
 
 

time: 32.3 us -> 30.6 us (0.947)
  local copies, waits for them, and re-layouts: 2.13 us -> 0.65 us
    unnamed x4 -> x2, local copies, waits for them, and re-layouts: 2.13 us -> 0.65 us
    pallas_call x1, Pallas kernels: 29.4 us -> 28.2 us  [per_device(): pl.pallas_call(functools.partial(update_kernel, na, ny, nz), out_shape=(j...]
    pallas_call x0 -> x1, Pallas kernels: none -> 1.01 us  [per_device(): pl.pallas_call(finish_kernel, out_shape=(jax.ShapeDtypeStruct((K, cols),...]
where the time goes in v3:
time: 30.6 us
  Pallas kernels  29.3 us (96%)
  local copies, waits for them, and re-layouts  0.65 us (2%)
  between operations  0.65 us (2%)
    pallas_call x1, Pallas kernels, per_device(): pl.pallas_call(functools.partial(update_kernel, na, ny, nz), out_shape=(j...  28.2 us
    pallas_call x1, Pallas kernels, per_device(): pl.pallas_call(finish_kernel, out_shape=(jax.ShapeDtypeStruct((K, cols),...  1.01 us
    unnamed x2, local copies, waits for them, and re-layouts  0.65 us

profile of v3, /device:TPU:1, one launch (start us, length us, event | category | flops | bytes accessed | tf_op | source)
XLA Modules:
  0.0 30.6 jit_solution(6946239272626399232)
XLA Ops:
  0.6 0.0 copy-start
  0.6 0.6 %copy-done = f32[32]{0:T(128)S(1)} copy-done((f32[32]{0:T(128)S(1)}, f32[32]{0:T(128)}, u32[]{:S(2)}) %copy-start) | copy-done | bytes 152
  1.3 28.2 %pod_update.1 = (f32[32,8192]{1,0:T(8,128)S(1)}, f32[1,32]{1,0:T(1,128)S(1)}) custom-call(f32[32,8192]{1,0:T(8,128)} %basis_hbm.1, f32[1,32]{1,0:T(1,128)S(1)} %bitcast.2, f32[64,8192]{1,0:T(8,128)} %snap_hbm.1), custom_call_target="tpu_custom_call" | custom-call | tf_op jit(solution)/shard_map/pod_update/pallas_call | solution.py:268
  29.5 1.0 %write_out.1 = (f32[32,8192]{1,0:T(8,128)}, f32[1,32]{1,0:T(1,128)}) custom-call(f32[32,8192]{1,0:T(8,128)S(1)} %get-tuple-element.6.modes_ref, f32[1,32]{1,0:T(1,128)S(1)} %get-tuple-element.7.values_ref), custom_call_target="tpu_custom_call" | custom-call | tf_op jit(solution)/shard_map/write_out/pallas_call | solution.py:290
Async XLA Ops:
  0.6 0.7 %copy-start = (f32[32]{0:T(128)S(1)}, f32[32]{0:T(128)}, u32[]{:S(2)}) copy-start(f32[32]{0:T(128)} %param.4) | copy-start | bytes 388

commit v4 on v3

--- a/solution.py
+++ b/solution.py
@@ -65,12 +65,15 @@
         out.append(Ub[kb] * wide(scale, L))
     return jnp.concatenate(out, axis=0)
 
-def dense(gbb, f, gss, sigma_row):
+def project(gbb, f):
     ft = f.T
     t = dot(gbb, f)
     c = 2.0*f - t
     ct = 2.0*ft - dot(ft, gbb)
-    h = dot(gbb, c) - f
+    return ft, c, ct, dot(gbb, c) - f
+
+
+def dense(ft, c, ct, h, gss, sigma_row):
     gram = gss + dot(jnp.concatenate([ct, -ft], 1), jnp.concatenate([h, c], 0))
     eye = lax.broadcasted_iota(jnp.int32, (K, K), 0) == lax.broadcasted_iota(jnp.int32, (K, K), 1)
     eye2 = lax.broadcasted_iota(jnp.int32, (NEW, NEW), 0) == lax.broadcasted_iota(jnp.int32, (NEW, NEW), 1)
@@ -141,6 +144,7 @@
     x, y, z = lax.axis_index("gx"), lax.axis_index("gy"), lax.axis_index("gz")
     deep = na // 2
     level, core = x // 2, lax.rem(x, 2)
+    own = 1 - core
     cols = basis_v.shape[1]
     loads = []
     for i in range(cols // LOAD):
@@ -155,15 +159,16 @@
     sigma_load = pltpu.make_async_copy(sigma_hbm, sigma_ref, sigma_sem)
     sigma_load.start()
 
-    def hops(d, n):
-        return min(d, n - d)
+    here = y * nz + z
+
+    def others_of(me, n):
+        return [k + (k - me + n) // n for k in range(n - 1)]
 
     other = {"gx": x + 1 - 2 * core}
-    plane = [(hops(dy, ny) + hops(dz, nz), {"gy": lax.rem(y + dy, ny), "gz": lax.rem(z + dz, nz)})
-             for dy in range(ny) for dz in range(nz) if dy or dz]
-    line = [(hops(d, deep), {"gx": lax.rem(level + d, deep) * 2 + core}) for d in range(1, deep)]
+    plane = [{"gy": t // nz, "gz": lax.rem(t, nz)} for t in others_of(here, ny * nz)]
+    line = [{"gx": 2 * t + core} for t in others_of(level, deep)]
     barrier = pltpu.get_barrier_semaphore()
-    for device in [other] + [d for _, d in plane + line]:
+    for device in [other] + plane + line:
         pl.semaphore_signal(barrier, inc=1, device_id=device, device_id_type=MESH)
 
     gram = split_gram(loads, basis_v, snap_v, split_v)
@@ -189,42 +194,51 @@
     def sent(phase, ref):
         pltpu.make_async_copy(ref, ref, send_sems.at[phase]).wait()
 
-    here = y * nz + z
     some_plane, some_line = pl.ds(0, len(plane)), pl.ds(0, len(line))
-    send(0, packed.at[1 - core], partner, other)
+    send(0, packed.at[1 - own], partner, other)
     arrive(0, partner)
     for i in range(2):
-        chip[i] = packed[core, i] + partner[i]
-    for far, which, device in sorted(
-            [(far, 0, device) for far, device in plane] + [(far, 1, device) for far, device in line],
-            key=lambda entry: -entry[0]):
+        chip[i] = packed[own, i] + partner[i]
+    order = [(k / len(plane), 0, k) for k in range(len(plane))] + [(k / len(line), 1, k) for k in range(len(line))]
+    for _, which, k in sorted(order):
         if which == 0:
-            send(1, chip.at[0], s1a.at[here], device)
+            send(1, chip.at[0], s1a.at[here], plane[k])
         else:
-            send(2, chip.at[1], s1b.at[level], device)
+            send(2, chip.at[1], s1b.at[level], line[k])
     s1a[here] = chip[0]
     s1b[level] = chip[1]
     arrive(2, s1b.at[some_line])
     mids[1] = tree_sum([s1b[i] for i in range(deep)])
-    for far, device in sorted(plane, key=lambda entry: -entry[0]):
+    for device in plane:
         send(3, mids.at[1], s2b.at[here], device)
     s2b[here] = mids[1]
     arrive(1, s1a.at[some_plane])
     mids[0] = tree_sum([s1a[i] for i in range(ny * nz)])
-    for far, device in sorted(line, key=lambda entry: -entry[0]):
+    for device in line:
         send(4, mids.at[0], s2a.at[level], device)
     s2a[level] = mids[0]
     arrive(4, s2a.at[some_line])
-    gathered[core, 0] = tree_sum([s2a[i] for i in range(deep)])
+    gathered[own, 0] = tree_sum([s2a[i] for i in range(deep)])
     arrive(3, s2b.at[some_plane])
-    gathered[core, 1] = tree_sum([s2b[i] for i in range(ny * nz)])
-    send(5, gathered.at[core], gathered.at[core], other)
-    arrive(5, gathered.at[1 - core])
+    gathered[own, 1] = tree_sum([s2b[i] for i in range(ny * nz)])
+    send(5, gathered.at[own], gathered.at[own], other)
+    scale = 1.0 / (cols * na * ny * nz)
+
+    @pl.when(core == 0)
+    def _():
+        arrive(5, gathered.at[0])
+
+    upper = jnp.concatenate([gathered[0, 0], gathered[0, 1]], axis=0) * scale
+    projected = project(upper[:, :K], upper[:, K:K + NEW])
+
+    @pl.when(core == 1)
+    def _():
+        arrive(5, gathered.at[1])
+
     sigma_load.wait()
-    upper = jnp.concatenate([gathered[0, 0], gathered[0, 1]], axis=0) * (1.0 / (cols * na * ny * nz))
-    lower = jnp.concatenate([gathered[1, 0], gathered[1, 1]], axis=0) * (1.0 / (cols * na * ny * nz))
+    lower = jnp.concatenate([gathered[1, 0], gathered[1, 1]], axis=0) * scale
     gss = jnp.concatenate([lower[:, :NEW], lower[:, NEW:]], axis=0)
-    coef, values = dense(upper[:, :K], upper[:, K:K + NEW], gss, sigma_ref[...])
+    coef, values = dense(*projected, gss, sigma_ref[...])
     eye = lax.broadcasted_iota(jnp.int32, (K, K), 0) == lax.broadcasted_iota(jnp.int32, (K, K), 1)
     values_ref[...] = jnp.sum(jnp.where(eye, values, 0.0), axis=0, keepdims=True)
     coef = coef[:, :K + NEW]

time: 30.6 us -> 30.1 us (0.984)
  Pallas kernels: 29.3 us -> 28.7 us
    pallas_call x1, Pallas kernels: 28.2 us -> 27.7 us  [per_device(): pl.pallas_call(functools.partial(update_kernel, na, ny, nz), out_shape=(j...]
where the time goes in v4:
time: 30.1 us; the launch traced here: 30 us
  Pallas kernels  28.7 us (95%)
  local copies, waits for them, and re-layouts  0.65 us (2%)
  between operations  0.65 us (2%)
    pallas_call x1, Pallas kernels, per_device(): pl.pallas_call(functools.partial(update_kernel, na, ny, nz), out_shape=(j...  27.7 us
    pallas_call x1, Pallas kernels, per_device(): pl.pallas_call(finish_kernel, out_shape=(jax.ShapeDtypeStruct((K, cols),...  1.01 us
    unnamed x2, local copies, waits for them, and re-layouts  0.65 us

profile of v4, /device:TPU:1, one launch (start us, length us, event | category | flops | bytes accessed | tf_op | source)
XLA Modules:
  0.0 30.0 jit_solution(18437078178678753930)
XLA Ops:
  0.6 0.0 copy-start
  0.6 0.6 %copy-done = f32[32]{0:T(128)S(1)} copy-done((f32[32]{0:T(128)S(1)}, f32[32]{0:T(128)}, u32[]{:S(2)}) %copy-start) | copy-done | bytes 152
  1.3 27.7 %pod_update.1 = (f32[32,8192]{1,0:T(8,128)S(1)}, f32[1,32]{1,0:T(1,128)S(1)}) custom-call(f32[32,8192]{1,0:T(8,128)} %basis_hbm.1, f32[1,32]{1,0:T(1,128)S(1)} %bitcast.2, f32[64,8192]{1,0:T(8,128)} %snap_hbm.1), custom_call_target="tpu_custom_call" | custom-call | tf_op jit(solution)/shard_map/pod_update/pallas_call | solution.py:282
  29.0 1.0 %write_out.1 = (f32[32,8192]{1,0:T(8,128)}, f32[1,32]{1,0:T(1,128)}) custom-call(f32[32,8192]{1,0:T(8,128)S(1)} %get-tuple-element.6.modes_ref, f32[1,32]{1,0:T(1,128)S(1)} %get-tuple-element.7.values_ref), custom_call_target="tpu_custom_call" | custom-call | tf_op jit(solution)/shard_map/write_out/pallas_call | solution.py:304
Async XLA Ops:
  0.6 0.7 %copy-start = (f32[32]{0:T(128)S(1)}, f32[32]{0:T(128)}, u32[]{:S(2)}) copy-start(f32[32]{0:T(128)} %param.4) | copy-start | bytes 388

commit v5 on v4

--- a/solution.py
+++ b/solution.py
@@ -107,9 +107,8 @@
     return U[:, :128], values
 
 
-CHUNK = 2048
+CHUNK = 1024
 LOAD = 2048
-PARTS = 4
 STACK = 2 * (K + NEW)
 
 
@@ -138,8 +137,8 @@
     return (full[:half, :half] + full[half:, half:]) + (full[half:, :half] + full[:half, half:])
 
 
-def update_kernel(na, ny, nz, basis_hbm, sigma_hbm, snap_hbm, modes_ref, values_ref,
-                basis_v, snap_v, split_v, packed, partner, chip, s1a, s1b, s2a, s2b, mids, gathered,
+def update_kernel(na, ny, nz, basis_hbm, sigma_hbm, snap_hbm, left_ref, values_ref, split_v,
+                basis_v, snap_v, packed, partner, chip, s1a, s1b, s2a, s2b, mids, gathered,
                 sigma_ref, sigma_sem, load_sems, send_sems, recv_sems):
     x, y, z = lax.axis_index("gx"), lax.axis_index("gy"), lax.axis_index("gz")
     deep = na // 2
@@ -244,12 +243,8 @@
     coef = coef[:, :K + NEW]
     high = coef.astype(jnp.bfloat16).astype(jnp.float32)
     rest = coef - high
-    left = jnp.concatenate([
+    left_ref[...] = jnp.concatenate([
         jnp.concatenate([high, high], axis=1), jnp.concatenate([rest, rest], axis=1)], axis=0).astype(jnp.bfloat16)
-    for i in range(cols // CHUNK):
-        at = slice(i * CHUNK, (i + 1) * CHUNK)
-        both = jnp.dot(left, split_v[:, at], preferred_element_type=jnp.float32)
-        modes_ref[:, at] = both[:K] + both[K:]
     sent(0, partner)
     sent(1, s1a.at[some_plane])
     sent(2, s1b.at[some_line])
@@ -258,14 +253,17 @@
     sent(5, partner)
 
 
-def finish_kernel(modes_ref, values_ref, modes_hbm, values_hbm, sems):
+def finish_kernel(left_ref, values_ref, split_ref, modes_hbm, values_hbm, modes_v, sems):
     cols = modes_hbm.shape[1]
-    parts = sems.shape[0] - 1
-    copies = [pltpu.make_async_copy(values_ref, values_hbm, sems.at[parts])]
+    chunks = cols // CHUNK
+    left = left_ref[...]
+    copies = [pltpu.make_async_copy(values_ref, values_hbm, sems.at[chunks])]
     copies[0].start()
-    for i in range(parts):
-        at = pl.ds(i * (cols // parts), cols // parts)
-        copies.append(pltpu.make_async_copy(modes_ref.at[:, at], modes_hbm.at[:, at], sems.at[i]))
+    for i in range(chunks):
+        at = pl.ds(i * CHUNK, CHUNK)
+        both = jnp.dot(left, split_ref[:, at], preferred_element_type=jnp.float32)
+        modes_v[:, at] = both[:K] + both[K:]
+        copies.append(pltpu.make_async_copy(modes_v.at[:, at], modes_hbm.at[:, at], sems.at[i]))
         copies[-1].start()
     for copy in copies:
         copy.wait()
@@ -279,16 +277,16 @@
     quarter = (K // 2, 128)
     def slots(*count):
         return pltpu.VMEM(count + quarter, jnp.float32)
-    modes, values = pl.pallas_call(
+    left, values, split = pl.pallas_call(
         functools.partial(update_kernel, na, ny, nz),
-        out_shape=(jax.ShapeDtypeStruct((K, cols), jnp.float32),
-                   jax.ShapeDtypeStruct((1, K), jnp.float32)),
+        out_shape=(jax.ShapeDtypeStruct((2 * K, STACK), jnp.bfloat16),
+                   jax.ShapeDtypeStruct((1, K), jnp.float32),
+                   jax.ShapeDtypeStruct((STACK, cols), jnp.bfloat16)),
         in_specs=[hbm, hbm, hbm],
-        out_specs=(vmem, vmem),
+        out_specs=(vmem, vmem, vmem),
         scratch_shapes=[
             pltpu.VMEM((K, cols), jnp.float32),
             pltpu.VMEM((NEW, cols), jnp.float32),
-            pltpu.VMEM((STACK, cols), jnp.bfloat16),
             slots(2, 2), slots(2), slots(2),
             slots(ny * nz), slots(na // 2), slots(na // 2), slots(ny * nz), slots(2), slots(2, 2),
             pltpu.VMEM((1, K), jnp.float32),
@@ -298,19 +296,20 @@
             pltpu.SemaphoreType.DMA((6,)),
         ],
         compiler_params=pltpu.CompilerParams(
-            collective_id=0, has_side_effects=True, vmem_limit_bytes=52 * 1024 * 1024),
+            collective_id=0, has_side_effects=True, vmem_limit_bytes=32 * 1024 * 1024),
         name="pod_update",
-    )(basis, sigma.reshape(1, K), snapshots)
+    )(*(pltpu.with_memory_space_constraint(value, pltpu.HBM)
+        for value in (basis, sigma.reshape(1, K), snapshots)))
     modes, values = pl.pallas_call(
         finish_kernel,
         out_shape=(jax.ShapeDtypeStruct((K, cols), jnp.float32),
                    jax.ShapeDtypeStruct((1, K), jnp.float32)),
-        in_specs=[pl.BlockSpec(memory_space=pl.ANY), vmem],
+        in_specs=[vmem, vmem, vmem],
         out_specs=(hbm, hbm),
-        scratch_shapes=[pltpu.SemaphoreType.DMA((PARTS + 1,))],
-        compiler_params=pltpu.CompilerParams(vmem_limit_bytes=1024 * 1024),
-        name="write_out",
-    )(modes, values)
+        scratch_shapes=[pltpu.VMEM((K, cols), jnp.float32), pltpu.SemaphoreType.DMA((cols // CHUNK + 1,))],
+        compiler_params=pltpu.CompilerParams(vmem_limit_bytes=8 * 1024 * 1024),
+        name="modes_product",
+    )(left, values, split)
     return modes, values.reshape(K)
 
 

time: 30.1 us -> 28.9 us (0.960)
  local copies, waits for them, and re-layouts: 0.65 us -> 0 us
  Pallas kernels: 28.7 us -> 28.2 us
    pallas_call x1, Pallas kernels: 27.7 us -> 26.7 us  [per_device(): pl.pallas_call(functools.partial(update_kernel, na, ny, nz), out_shape=(j...]
    unnamed x2 -> x0, local copies, waits for them, and re-layouts: 0.65 us -> none
    pallas_call x1, Pallas kernels: 1.01 us -> 1.44 us  [per_device(): pl.pallas_call(finish_kernel, out_shape=(jax.ShapeDtypeStruct((K, cols),...]
where the time goes in v5:
time: 28.9 us; the launch traced here: 28.8 us
  Pallas kernels  28.2 us (98%)
  between operations  0.64 us (2%)
    pallas_call x1, Pallas kernels, per_device(): pl.pallas_call(functools.partial(update_kernel, na, ny, nz), out_shape=(j...  26.7 us
    pallas_call x1, Pallas kernels, per_device(): pl.pallas_call(finish_kernel, out_shape=(jax.ShapeDtypeStruct((K, cols),...  1.44 us

profile of v5, /device:TPU:1, one launch (start us, length us, event | category | flops | bytes accessed | tf_op | source)
XLA Modules:
  0.0 28.8 jit_solution(16983545930360594177)
XLA Ops:
  0.6 26.7 %pod_update.1 = (bf16[64,192]{1,0:T(8,128)(2,1)S(1)}, f32[1,32]{1,0:T(1,128)S(1)}, bf16[192,8192]{1,0:T(8,128)(2,1)S(1)}) custom-call(f32[32,8192]{1,0:T(8,128)} %basis_hbm.1, f32[1,32]{1,0:T(1,128)} %bitcast.2, f32[64,8192]{1,0:T(8,128)} %snap_hbm.1), custom_call_target="tpu_custom_call" | custom-call | tf_op jit(solution)/shard_map/pod_update/pallas_call | solution.py:280
  27.4 1.4 %modes_product.1 = (f32[32,8192]{1,0:T(8,128)}, f32[1,32]{1,0:T(1,128)}) custom-call(bf16[64,192]{1,0:T(8,128)(2,1)S(1)} %get-tuple-element.7.left_ref, f32[1,32]{1,0:T(1,128)S(1)} %get-tuple-element.8.values_ref, bf16[192,8192]{1,0:T(8,128)(2,1)S(1)} %get-tuple-element.9.split_ref), custom_call_target="tpu_custom_call" | custom-call | tf_op jit(solution)/shard_map/modes_product/pallas_call | solution.py:303

commit v6 on v5

--- a/solution.py
+++ b/solution.py
@@ -108,7 +108,7 @@
 
 
 CHUNK = 1024
-LOAD = 2048
+LOAD = 4096
 STACK = 2 * (K + NEW)
 
 
@@ -118,21 +118,20 @@
     return values[0]
 
 
-def split_gram(loads, basis_v, snap_v, split_v):
-    full = None
-    for i, pair in enumerate(loads):
-        for copy in pair:
-            copy.wait()
-        at = slice(i * LOAD, (i + 1) * LOAD)
-        for ref, low in ((basis_v, 0), (snap_v, K)):
+def split_gram(load_sems, basis_v, snap_v, split_v):
+    def step(i, full):
+        at = pl.ds(pl.multiple_of(i * LOAD, LOAD), LOAD)
+        for which, ref, low in ((0, basis_v, 0), (1, snap_v, K)):
+            pltpu.make_async_copy(ref.at[:, at], ref.at[:, at], load_sems.at[which, i]).wait()
             value = ref[:, at]
             high = value.astype(jnp.bfloat16)
             rest = (value - high.astype(jnp.float32)).astype(jnp.bfloat16)
             split_v[low:low + value.shape[0], at] = high
             split_v[K + NEW + low:K + NEW + low + value.shape[0], at] = rest
         both = split_v[:, at]
-        term = lax.dot_general(both, both, (((1,), (1,)), ((), ())), preferred_element_type=jnp.float32)
-        full = term if full is None else full + term
+        return full + lax.dot_general(both, both, (((1,), (1,)), ((), ())), preferred_element_type=jnp.float32)
+
+    full = lax.fori_loop(0, basis_v.shape[1] // LOAD, step, jnp.zeros((STACK, STACK), jnp.float32))
     half = K + NEW
     return (full[:half, :half] + full[half:, half:]) + (full[half:, :half] + full[:half, half:])
 
@@ -166,11 +165,18 @@
     other = {"gx": x + 1 - 2 * core}
     plane = [{"gy": t // nz, "gz": lax.rem(t, nz)} for t in others_of(here, ny * nz)]
     line = [{"gx": 2 * t + core} for t in others_of(level, deep)]
+    def hops(d, n):
+        return min(d, n - d)
+
+    far = [(hops(dy, ny) + hops(dz, nz), {"gy": lax.rem(y + dy, ny), "gz": lax.rem(z + dz, nz)})
+           for dy in range(ny) for dz in range(nz) if dy or dz]
+    far += [(hops(d, deep), {"gx": lax.rem(level + d, deep) * 2 + core}) for d in range(1, deep)]
+    far = [device for _, device in sorted(far, key=lambda entry: -entry[0])]
     barrier = pltpu.get_barrier_semaphore()
-    for device in [other] + plane + line:
+    for device in far + [other]:
         pl.semaphore_signal(barrier, inc=1, device_id=device, device_id_type=MESH)
 
-    gram = split_gram(loads, basis_v, snap_v, split_v)
+    gram = split_gram(load_sems, basis_v, snap_v, split_v)
     half = K + NEW
     gap = jnp.zeros((K, 128 - half), jnp.float32)
     upper = jnp.concatenate([gram[:K], gap], axis=1)

time: 28.9 us -> 28.5 us (0.986)
  Pallas kernels: 28.2 us -> 27.8 us
    pallas_call x1, Pallas kernels: 26.7 us -> 26.4 us  [per_device(): pl.pallas_call(functools.partial(update_kernel, na, ny, nz), out_shape=(j...]
where the time goes in v6:
time: 28.5 us
  Pallas kernels  27.8 us (98%)
  between operations  0.64 us (2%)
    pallas_call x1, Pallas kernels, per_device(): pl.pallas_call(functools.partial(update_kernel, na, ny, nz), out_shape=(j...  26.4 us
    pallas_call x1, Pallas kernels, per_device(): pl.pallas_call(finish_kernel, out_shape=(jax.ShapeDtypeStruct((K, cols),...  1.45 us

profile of v6, /device:TPU:1, one launch (start us, length us, event | category | flops | bytes accessed | tf_op | source)
XLA Modules:
  0.0 28.5 jit_solution(8935276206039191882)
XLA Ops:
  0.6 26.4 %pod_update.1 = (bf16[64,192]{1,0:T(8,128)(2,1)S(1)}, f32[1,32]{1,0:T(1,128)S(1)}, bf16[192,8192]{1,0:T(8,128)(2,1)S(1)}) custom-call(f32[32,8192]{1,0:T(8,128)} %basis_hbm.1, f32[1,32]{1,0:T(1,128)} %bitcast.2, f32[64,8192]{1,0:T(8,128)} %snap_hbm.1), custom_call_target="tpu_custom_call" | custom-call | tf_op jit(solution)/shard_map/pod_update/pallas_call | solution.py:286
  27.0 1.4 %modes_product.1 = (f32[32,8192]{1,0:T(8,128)}, f32[1,32]{1,0:T(1,128)}) custom-call(bf16[64,192]{1,0:T(8,128)(2,1)S(1)} %get-tuple-element.7.left_ref, f32[1,32]{1,0:T(1,128)S(1)} %get-tuple-element.8.values_ref, bf16[192,8192]{1,0:T(8,128)(2,1)S(1)} %get-tuple-element.9.split_ref), custom_call_target="tpu_custom_call" | custom-call | tf_op jit(solution)/shard_map/modes_product/pallas_call | solution.py:309

commit v7 on v6

--- a/solution.py
+++ b/solution.py
@@ -49,15 +49,15 @@
             for j in range(r+2, 8):
                 xa = spread(X[j, kb], r); xb = spread(X[j, kb], r+1)
                 for i in range(kb, nb):
-                    X[j, i] = X[j, i] - f1[i]*xa - f2[i]*xb
+                    X[j, i] = X[j, i] - (f1[i]*xa + f2[i]*xb)
             for j in range(8 if ahead else 0):
                 xa = spread(X[r, kb+1], j); xb = spread(X[r+1, kb+1], j)
                 for i in range(kb+1, nb):
-                    ahead[j, i] = ahead[j, i] - f1[i]*xa - f2[i]*xb
+                    ahead[j, i] = ahead[j, i] - (f1[i]*xa + f2[i]*xb)
             na = spread(Nb[kb], r); nbb = spread(Nb[kb], r+1)
             ua = spread(Ub[kb], r); ub = spread(Ub[kb], r+1)
             for i in range(kb, nb):
-                if kb < nb-1:
+                if kb < nb-1 and (r < 2 or kb < nb-2) and (i > kb or r < 6):
                     w = Nb[i].shape[1]
                     Nb[i] = Nb[i] - wide(f1[i], w)*na - wide(f2[i], w)*nbb
                 Ub[i] = Ub[i] - wide(f1[i], L)*ua - wide(f2[i], L)*ub

time: 28.5 us -> 28.5 us (level)
  no operation moved by 1% of the time
where the time goes in v7:
time: 28.5 us
  Pallas kernels  27.8 us (98%)
  between operations  0.64 us (2%)
    pallas_call x1, Pallas kernels, per_device(): pl.pallas_call(functools.partial(update_kernel, na, ny, nz), out_shape=(j...  26.4 us
    pallas_call x1, Pallas kernels, per_device(): pl.pallas_call(finish_kernel, out_shape=(jax.ShapeDtypeStruct((K, cols),...  1.45 us

profile of v7, /device:TPU:1, one launch (start us, length us, event | category | flops | bytes accessed | tf_op | source)
XLA Modules:
  0.0 28.5 jit_solution(18102147186728772581)
XLA Ops:
  0.6 26.4 %pod_update.1 = (bf16[64,192]{1,0:T(8,128)(2,1)S(1)}, f32[1,32]{1,0:T(1,128)S(1)}, bf16[192,8192]{1,0:T(8,128)(2,1)S(1)}) custom-call(f32[32,8192]{1,0:T(8,128)} %basis_hbm.1, f32[1,32]{1,0:T(1,128)} %bitcast.2, f32[64,8192]{1,0:T(8,128)} %snap_hbm.1), custom_call_target="tpu_custom_call" | custom-call | tf_op jit(solution)/shard_map/pod_update/pallas_call | solution.py:286
  27.0 1.4 %modes_product.1 = (f32[32,8192]{1,0:T(8,128)}, f32[1,32]{1,0:T(1,128)}) custom-call(bf16[64,192]{1,0:T(8,128)(2,1)S(1)} %get-tuple-element.7.left_ref, f32[1,32]{1,0:T(1,128)S(1)} %get-tuple-element.8.values_ref, bf16[192,8192]{1,0:T(8,128)(2,1)S(1)} %get-tuple-element.9.split_ref), custom_call_target="tpu_custom_call" | custom-call | tf_op jit(solution)/shard_map/modes_product/pallas_call | solution.py:309
